TPU v7x, 32 devices: a whole 2x2x4 slice. The times are simulated.
32 devices in a mesh: ctx: 8 (over y, x, core), ch: 4 (over z).
Axes of the slice: x: 2, y: 2, z: 4, core: 2. Of those that a mesh axis runs over, the one named last changes fastest.
Arguments:
- signal: bfloat16 [128, 131072], P('ch', 'ctx'), parts along dimension 0, may hold values from -6 to 6
- filter_taps: float32 [128, 131072], P('ch', 'ctx'), parts along dimension 0, may hold values from -0.015625 to 0.015625
- gate_values: bfloat16 [128, 131072], P('ch', 'ctx'), parts along dimension 0, may hold values from -6 to 6
- skip_gain: float32 [128], P('ch'), parts along dimension 0, may hold values from -4 to 4
Outputs:
- gated_output: bfloat16 [128, 131072], P('ch', 'ctx'), parts along dimension 0
There are 4 independent parts, one for each index of `ch`. A program takes and returns all parts, laid end to end along the dimension named above; each array names one. Nothing has to cross between parts.
All inputs are finite; a program needn't handle non-finite values.
Results may differ from a plain program's by a relative error of at most 0.001.
Values sent between devices are 32-bit elements; how exact they have to be, the bound alone decides.
A program may use at most 128 MiB of HBM per device.

v0:
```python
import functools
import math

import jax
import jax.numpy as jnp
import ml_dtypes
import numpy as np
from jax import lax
from jax.experimental import pallas as pl
from jax.experimental.pallas import tpu as pltpu
from jax.sharding import PartitionSpec as P

MESH = pl.DeviceIdType.MESH
BF16 = jnp.bfloat16
F32 = jnp.float32


def split_table(values):
    high = values.astype(ml_dtypes.bfloat16)
    low = (values - high.astype(np.float64)).astype(ml_dtypes.bfloat16)
    return high, low


def angles(rows, columns, period):
    return 2.0 * math.pi / period * (np.outer(rows, columns) % period)


def make_tables(first_len, second_len, chunk):
    chunks = first_len // chunk
    length = first_len * second_len
    first = np.arange(first_len, dtype=np.int64)
    second = np.arange(second_len, dtype=np.int64)
    quarter = 4 * first + 1
    theta = angles(quarter, first, 4 * first_len)
    forward = np.stack([np.cos(theta), -np.sin(theta)]).reshape(2, chunks, chunk, first_len)
    forward = forward.transpose(1, 0, 2, 3).reshape(chunks, 2 * chunk, first_len)
    backward = np.ascontiguousarray(forward.transpose(0, 2, 1))
    theta = angles(quarter, second, 4 * length)
    twist = np.stack([np.cos(theta), -np.sin(theta)]).reshape(2, chunks, chunk, second_len)
    twist = np.ascontiguousarray(twist.transpose(1, 0, 2, 3)).astype(np.float32)
    theta = angles(second, second, second_len)
    cos, sin = np.cos(theta), np.sin(theta)
    inner = np.block([[cos, -sin], [sin, cos]])
    return (*split_table(forward), *split_table(backward), *split_table(inner), twist)


def split(values):
    high = values.astype(BF16)
    low = (values - high.astype(F32)).astype(BF16)
    return high, low


def dot(left, right):
    return jnp.dot(left, right, preferred_element_type=F32)


def kernel(devices, chunk, sf_ref, *refs):
    tables, (out_ref,), rest = refs[:7], refs[7:8], refs[8:]
    held, rest = rest[:7], rest[7:]
    got, wide, send_sem, recv_sem, own_sem, table_sem, back_send, back_recv, back_own = rest
    fwd_hi, fwd_lo, bwd_hi, bwd_lo, in_hi, in_lo, twist = held
    me = lax.axis_index("ctx")
    _, channels, _, rows, width = sf_ref.shape
    chunks = fwd_hi.shape[0]
    scale = 1.0 / (devices * rows * width)

    def peer(step):
        return lax.rem(me + step, devices)

    barrier = pltpu.get_barrier_semaphore()
    for step in range(1, devices):
        pl.semaphore_signal(barrier, inc=1, device_id={"ctx": peer(step)}, device_id_type=MESH)
    pl.semaphore_wait(barrier, devices - 1)

    def own_rows(device):
        return pl.ds(pl.multiple_of(device * rows, rows), rows)

    def outward(channel, step):
        return pltpu.make_async_remote_copy(
            src_ref=sf_ref.at[peer(step), channel],
            dst_ref=got.at[channel, :, own_rows(me), :],
            send_sem=send_sem.at[channel, step],
            recv_sem=recv_sem.at[channel, step],
            device_id={"ctx": peer(step)},
            device_id_type=MESH,
        )

    def outward_own(channel):
        return pltpu.make_async_copy(
            sf_ref.at[me, channel], got.at[channel, :, own_rows(me), :], own_sem.at[channel]
        )

    def inward(channel, step):
        return pltpu.make_async_remote_copy(
            src_ref=got.at[channel, 0, own_rows(peer(step)), :],
            dst_ref=out_ref.at[me, channel],
            send_sem=back_send.at[channel, step],
            recv_sem=back_recv.at[channel, step],
            device_id={"ctx": peer(step)},
            device_id_type=MESH,
        )

    def inward_own(channel):
        return pltpu.make_async_copy(
            got.at[channel, 0, own_rows(me), :], out_ref.at[me, channel], back_own.at[channel]
        )

    for channel in range(channels):
        for step in range(1, devices):
            outward(channel, step).start()
        outward_own(channel).start()
    loads = [
        pltpu.make_async_copy(source, target, table_sem.at[i])
        for i, (source, target) in enumerate(zip(tables, held))
    ]
    for load in loads:
        load.start()
    for load in loads:
        load.wait()

    def one_channel(channel, carry):
        outward_own(channel).wait()
        for step in range(1, devices):
            outward(channel, step).wait_recv()
        high, low = split(got[channel, 1])
        wide[:, :width] = got[channel, 0].astype(BF16)
        wide[:, width : 2 * width] = high
        wide[:, 2 * width :] = low

        def one_chunk(part, carry):
            from_high = dot(fwd_hi[part], wide[...])
            from_low = dot(fwd_lo[part], wide[:, : 2 * width])
            both = from_high[:, : 2 * width] + from_low
            series = (both[:, :width], both[:, width:] + from_high[:, 2 * width :])
            cos, sin = twist[part, 0], twist[part, 1]
            turned = [
                jnp.concatenate(
                    [
                        value[:chunk] * cos - value[chunk:] * sin,
                        value[:chunk] * sin + value[chunk:] * cos,
                    ],
                    axis=1,
                )
                for value in series
            ]
            high, low = split(jnp.concatenate(turned, axis=0))
            bins = dot(high, in_hi[...]) + dot(high, in_lo[...]) + dot(low, in_hi[...])
            s_re, s_im = bins[:chunk, :width], bins[:chunk, width:]
            f_re, f_im = bins[chunk:, :width] * scale, bins[chunk:, width:] * scale
            prod = jnp.concatenate(
                [s_re * f_re - s_im * f_im, -(s_re * f_im + s_im * f_re)], axis=1
            )
            high, low = split(prod)
            back = dot(high, in_hi[...]) + dot(high, in_lo[...]) + dot(low, in_hi[...])
            b_re, b_im = back[:, :width], back[:, width:]
            high, low = split(
                jnp.concatenate([b_re * cos - b_im * sin, -(b_re * sin + b_im * cos)], axis=0)
            )
            term = dot(bwd_hi[part], high) + dot(bwd_lo[part], high) + dot(bwd_hi[part], low)

            @pl.when(part == 0)
            def _():
                got[channel, 0] = term

            @pl.when(part > 0)
            def _():
                got[channel, 0] += term

            return carry

        lax.fori_loop(0, chunks, one_chunk, 0)
        for step in range(1, devices):
            inward(channel, step).start()
        inward_own(channel).start()
        return carry

    lax.fori_loop(0, channels, one_channel, 0)
    for channel in range(channels):
        inward_own(channel).wait()
        for step in range(1, devices):
            outward(channel, step).wait_send()
            inward(channel, step).wait_send()
            inward(channel, step).wait_recv()


def shards(signal, filter_taps, gate_values, skip_gain):
    devices = lax.axis_size("ctx")
    channels, block = signal.shape
    length = devices * block
    own = channels // devices
    second_len = 1
    while 4 * second_len * second_len <= length:
        second_len *= 2
    first_len = length // second_len
    rows = first_len // devices
    chunk = min(first_len, max(128, 131072 // first_len))
    tables = make_tables(first_len, second_len, chunk)
    inputs = signal.astype(F32)
    shape = (devices, own, rows, second_len)
    packed = jnp.stack([inputs.reshape(shape), filter_taps.reshape(shape)], axis=2)
    anywhere = pl.BlockSpec(memory_space=pl.ANY)
    pairs = pltpu.SemaphoreType.DMA((own, devices))
    singles = pltpu.SemaphoreType.DMA((own,))
    long_conv = pl.pallas_call(
        functools.partial(kernel, devices, chunk),
        out_shape=jax.ShapeDtypeStruct(shape, F32),
        in_specs=[anywhere] * 8,
        out_specs=anywhere,
        scratch_shapes=[pltpu.VMEM(table.shape, table.dtype) for table in tables]
        + [
            pltpu.VMEM((own, 2, first_len, second_len), F32),
            pltpu.VMEM((first_len, 3 * second_len), BF16),
            pairs,
            pairs,
            singles,
            pltpu.SemaphoreType.DMA((7,)),
            pairs,
            pairs,
            singles,
        ],
        compiler_params=pltpu.CompilerParams(
            collective_id=0, has_side_effects=True, vmem_limit_bytes=60 * 1024 * 1024
        ),
    )(packed, *[jnp.asarray(table) for table in tables])
    long_conv = long_conv.reshape(channels, block)
    gated = gate_values.astype(F32) * (long_conv + skip_gain[:, None] * inputs)
    return gated.astype(BF16)


def solution(mesh):
    in_specs = (P("ch", "ctx"), P("ch", "ctx"), P("ch", "ctx"), P("ch"))
    out_specs = P("ch", "ctx")
    return jax.shard_map(shards, mesh=mesh, in_specs=in_specs, out_specs=out_specs, check_vma=False)
```

profile of v0, /device:TPU:1, one launch (start us, length us, event | category | flops | bytes accessed | tf_op | source)
XLA Modules:
  0.0 83.4 jit_solution(16333520485430523844)
XLA Ops:
  0.0 0.0 copy-start
  0.0 2.3 %copy.13 = f32[4,8,64,256]{3,2,1,0:T(8,128)S(1)} copy(f32[4,8,64,256]{3,1,2,0:T(8,128)} %bitcast.15) | data formatting | bytes 4194304
  2.3 0.0 copy-done
  2.3 0.3 copy.12
  2.6 2.2 %pad_maximum_fusion.sf_ref = f32[8,4,2,64,256]{4,3,2,1,0:T(8,128)} fusion(f32[8,4,1,64,256]{4,3,2,1,0:T(8,128)S(1)} %bitcast.12, f32[8,4,1,64,256]{4,3,2,1,0:T(8,128)S(1)} %bitcast.13), kind=kLoop, calls=%fused_computation | loop fusion | flops 1048576 | bytes 8388608 | tf_op jit(solution)/shard_map/stack | solution.py:200
  4.9 74.2 %shard_map.109 = f32[8,4,64,256]{3,2,1,0:T(8,128)} custom-call(f32[8,4,2,64,256]{4,3,2,1,0:T(8,128)} %pad_maximum_fusion.sf_ref, bf16[2,512,512]{2,1,0:T(8,128)(2,1)} %constant.14.clone.refs_0_, bf16[2,512,512]{2,1,0:T(8,128)(2,1)} %constant.15.clone.refs_1_, bf16[2,512,512]{2,1,0:T(8,128)(2,1)} %constant.16.clone.refs_2_, ...), custom_call_target="tpu_custom_call" | custom-call | tf_op jit(solution)/shard_map/pallas_call | solution.py:204
  79.0 0.0 copy-start.1
  79.1 0.0 copy-start.2
  79.1 2.9 %copy.14 = f32[4,8,64,256]{3,1,2,0:T(8,128)S(1)} copy(f32[4,8,64,256]{3,2,1,0:T(8,128)} %bitcast.11) | data formatting | bytes 4194304
  82.0 0.0 copy-done.1
  82.0 0.0 copy-done.2
  82.0 1.4 %multiply_convert_fusion = bf16[32,16384]{1,0:T(8,128)(2,1)} fusion(f32[32,16384]{1,0:T(8,128)S(1)} %bitcast.10, bf16[32,16384]{1,0:T(8,128)(2,1)S(1)} %copy-done.1, f32[32]{0:T(128)S(1)} %copy-done.2, bf16[32,16384]{1,0:T(8,128)(2,1)S(1)} %copy-done), kind=kLoop, calls=%fused_computation.1 | loop fusion | flops 3145728 | bytes 5243008 | tf_op jit(solution)/shard_map/convert_element_type | solution.py:227
Async XLA Ops:
  0.0 2.3 %copy-start = (bf16[32,16384]{1,0:T(8,128)(2,1)S(1)}, bf16[32,16384]{1,0:T(8,128)(2,1)}, u32[]{:S(2)}) copy-start(bf16[32,16384]{1,0:T(8,128)(2,1)} %param.11) | copy-start | bytes 3145732
  79.0 2.9 %copy-start.1 = (bf16[32,16384]{1,0:T(8,128)(2,1)S(1)}, bf16[32,16384]{1,0:T(8,128)(2,1)}, u32[]{:S(2)}) copy-start(bf16[32,16384]{1,0:T(8,128)(2,1)} %param.13) | copy-start | bytes 3145732
  79.1 2.9 %copy-start.2 = (f32[32]{0:T(128)S(1)}, f32[32]{0:T(128)}, u32[]{:S(2)}) copy-start(f32[32]{0:T(128)} %param.14) | copy-start | bytes 388
where the time goes:
time: 83.6 us; the launch traced here: 83.4 us
  Pallas kernels  74.2 us (89%)
  local copies, waits for them, and re-layouts  5.51 us (7%)
  other arithmetic  3.66 us (4%)
    pallas_call x1, Pallas kernels, shards(): pl.pallas_call(functools.partial(kernel, devices, chunk), out_shape=jax.S...  74.2 us
    unnamed x9, local copies, waits for them, and re-layouts  5.51 us
    another operation x1, other arithmetic, shards(): jnp.stack([inputs.reshape(shape), filter_taps.reshape(shape)], axis=2)  2.24 us

commit v1 on v0

--- a/solution.py
+++ b/solution.py
@@ -54,23 +54,68 @@
     return jnp.dot(left, right, preferred_element_type=F32)
 
 
-def kernel(devices, chunk, sf_ref, *refs):
-    tables, (out_ref,), rest = refs[:7], refs[7:8], refs[8:]
-    held, rest = rest[:7], rest[7:]
-    got, wide, send_sem, recv_sem, own_sem, table_sem, back_send, back_recv, back_own = rest
+def kernel(devices, chunk, fused, *refs):
+    tables, rest = refs[:7], refs[7:]
+    held = rest[-16:-9]
+    got, wide, send_sem, recv_sem, own_sem, table_sem, back_send, back_recv, back_own = rest[-9:]
+    if fused:
+        signal_ref, taps_ref, gate_ref, skip_ref, out_ref = rest[:5]
+        signal, taps, gate, result, tile_s, tile_f, sf_ref, back_ref, load_sem = rest[5:-16]
+    else:
+        sf_ref, back_ref = rest[:2]
     fwd_hi, fwd_lo, bwd_hi, bwd_lo, in_hi, in_lo, twist = held
     me = lax.axis_index("ctx")
     _, channels, _, rows, width = sf_ref.shape
     chunks = fwd_hi.shape[0]
     scale = 1.0 / (devices * rows * width)
+    folds = width // 128
+    lanes = devices * channels
 
     def peer(step):
         return lax.rem(me + step, devices)
+
+    if fused:
+        arrivals = [
+            pltpu.make_async_copy(source, target, load_sem.at[i])
+            for i, (source, target) in enumerate(
+                ((taps_ref, taps), (signal_ref, signal), (gate_ref, gate))
+            )
+        ]
+        for arrival in arrivals:
+            arrival.start()
 
     barrier = pltpu.get_barrier_semaphore()
     for step in range(1, devices):
         pl.semaphore_signal(barrier, inc=1, device_id={"ctx": peer(step)}, device_id_type=MESH)
+
+    def tile(column):
+        return pl.ds(pl.multiple_of(column * 128, 128), 128)
+
+    def tile_rows(column):
+        return pl.ds(pl.multiple_of(column * lanes, lanes), lanes)
+
+    if fused:
+        columns = rows * folds
+        arrivals[0].wait()
+
+        def lay_taps(column, carry):
+            tile_f[tile_rows(column), :] = taps[:, tile(column)]
+            return carry
+
+        lax.fori_loop(0, columns, lay_taps, 0, unroll=8)
+        arrivals[1].wait()
+
+        def lay_signal(column, carry):
+            tile_s[tile_rows(column), :] = signal[:, tile(column)].astype(F32)
+            return carry
+
+        lax.fori_loop(0, columns, lay_signal, 0, unroll=8)
+
     pl.semaphore_wait(barrier, devices - 1)
+
+    def strip(device, channel, fold):
+        start = device * channels + channel + fold * lanes
+        return pl.ds(start, rows, stride=lanes * folds)
 
     def own_rows(device):
         return pl.ds(pl.multiple_of(device * rows, rows), rows)
@@ -93,7 +138,7 @@
     def inward(channel, step):
         return pltpu.make_async_remote_copy(
             src_ref=got.at[channel, 0, own_rows(peer(step)), :],
-            dst_ref=out_ref.at[me, channel],
+            dst_ref=back_ref.at[me, channel],
             send_sem=back_send.at[channel, step],
             recv_sem=back_recv.at[channel, step],
             device_id={"ctx": peer(step)},
@@ -102,10 +147,17 @@
 
     def inward_own(channel):
         return pltpu.make_async_copy(
-            got.at[channel, 0, own_rows(me), :], out_ref.at[me, channel], back_own.at[channel]
+            got.at[channel, 0, own_rows(me), :], back_ref.at[me, channel], back_own.at[channel]
         )
 
     for channel in range(channels):
+        if fused:
+            for device in range(devices):
+                for fold in range(folds):
+                    part = pl.ds(fold * 128, 128)
+                    where = strip(device, channel, fold)
+                    sf_ref[device, channel, 0, :, part] = tile_s[where, :]
+                    sf_ref[device, channel, 1, :, part] = tile_f[where, :]
         for step in range(1, devices):
             outward(channel, step).start()
         outward_own(channel).start()
@@ -178,9 +230,29 @@
     for channel in range(channels):
         inward_own(channel).wait()
         for step in range(1, devices):
+            inward(channel, step).wait_recv()
+        if fused:
+            for device in range(devices):
+                for fold in range(folds):
+                    part = pl.ds(fold * 128, 128)
+                    tile_s[strip(device, channel, fold), :] = back_ref[device, channel, :, part]
+    if fused:
+        arrivals[2].wait()
+
+        def finish(column, carry):
+            there = tile(column)
+            total = tile_s[tile_rows(column), :] + skip_ref[...] * signal[:, there].astype(F32)
+            result[:, there] = (gate[:, there].astype(F32) * total).astype(BF16)
+            return carry
+
+        lax.fori_loop(0, columns, finish, 0, unroll=8)
+        leave = pltpu.make_async_copy(result, out_ref, load_sem.at[3])
+        leave.start()
+        leave.wait()
+    for channel in range(channels):
+        for step in range(1, devices):
             outward(channel, step).wait_send()
             inward(channel, step).wait_send()
-            inward(channel, step).wait_recv()
 
 
 def shards(signal, filter_taps, gate_values, skip_gain):
@@ -195,34 +267,57 @@
     rows = first_len // devices
     chunk = min(first_len, max(128, 131072 // first_len))
     tables = make_tables(first_len, second_len, chunk)
-    inputs = signal.astype(F32)
+    fused = channels * block <= 1 << 19
     shape = (devices, own, rows, second_len)
-    packed = jnp.stack([inputs.reshape(shape), filter_taps.reshape(shape)], axis=2)
+    packed_shape = (devices, own, 2, rows, second_len)
     anywhere = pl.BlockSpec(memory_space=pl.ANY)
     pairs = pltpu.SemaphoreType.DMA((own, devices))
     singles = pltpu.SemaphoreType.DMA((own,))
-    long_conv = pl.pallas_call(
-        functools.partial(kernel, devices, chunk),
-        out_shape=jax.ShapeDtypeStruct(shape, F32),
-        in_specs=[anywhere] * 8,
+    scratch = [pltpu.VMEM(table.shape, table.dtype) for table in tables] + [
+        pltpu.VMEM((own, 2, first_len, second_len), F32),
+        pltpu.VMEM((first_len, 3 * second_len), BF16),
+        pairs,
+        pairs,
+        singles,
+        pltpu.SemaphoreType.DMA((7,)),
+        pairs,
+        pairs,
+        singles,
+    ]
+    if fused:
+        scratch = [
+            pltpu.VMEM((channels, block), BF16),
+            pltpu.VMEM((channels, block), F32),
+            pltpu.VMEM((channels, block), BF16),
+            pltpu.VMEM((channels, block), BF16),
+            pltpu.VMEM((channels * block // 128, 128), F32),
+            pltpu.VMEM((channels * block // 128, 128), F32),
+            pltpu.VMEM(packed_shape, F32),
+            pltpu.VMEM(shape, F32),
+            pltpu.SemaphoreType.DMA((4,)),
+        ] + scratch
+        gains = jnp.broadcast_to(skip_gain[:, None], (channels, 128))
+        operands = [signal, filter_taps, gate_values, gains]
+        specs = [anywhere] * 3 + [pl.BlockSpec(memory_space=pltpu.VMEM)]
+        out_shape = jax.ShapeDtypeStruct((channels, block), BF16)
+    else:
+        inputs = signal.astype(F32)
+        operands = [jnp.stack([inputs.reshape(shape), filter_taps.reshape(shape)], axis=2)]
+        specs = [anywhere]
+        out_shape = jax.ShapeDtypeStruct(shape, F32)
+    result = pl.pallas_call(
+        functools.partial(kernel, devices, chunk, fused),
+        out_shape=out_shape,
+        in_specs=[anywhere] * 7 + specs,
         out_specs=anywhere,
-        scratch_shapes=[pltpu.VMEM(table.shape, table.dtype) for table in tables]
-        + [
-            pltpu.VMEM((own, 2, first_len, second_len), F32),
-            pltpu.VMEM((first_len, 3 * second_len), BF16),
-            pairs,
-            pairs,
-            singles,
-            pltpu.SemaphoreType.DMA((7,)),
-            pairs,
-            pairs,
-            singles,
-        ],
+        scratch_shapes=scratch,
         compiler_params=pltpu.CompilerParams(
             collective_id=0, has_side_effects=True, vmem_limit_bytes=60 * 1024 * 1024
         ),
-    )(packed, *[jnp.asarray(table) for table in tables])
-    long_conv = long_conv.reshape(channels, block)
+    )(*[jnp.asarray(table) for table in tables], *operands)
+    if fused:
+        return result
+    long_conv = result.reshape(channels, block)
     gated = gate_values.astype(F32) * (long_conv + skip_gain[:, None] * inputs)
     return gated.astype(BF16)
 

time: 83.6 us -> 82.2 us (0.983)
  Pallas kernels: 74.2 us -> 78.4 us
  other arithmetic: 3.66 us -> 0 us
  local copies, waits for them, and re-layouts: 5.51 us -> 3.59 us
    pallas_call x1, Pallas kernels: 74.2 us -> 78.4 us  [shards(): pl.pallas_call(functools.partial(kernel, devices, chunk, fused), out_shap...]
    unnamed x9 -> x1, local copies, waits for them, and re-layouts: 5.51 us -> 2.26 us
    another operation x1 -> x0, other arithmetic: 2.24 us -> none  [shards(): jnp.stack([inputs.reshape(shape), filter_taps.reshape(shape)], axis=2)]
    convert_element_type x1 -> x0, other arithmetic: 1.43 us -> none  [shards(): return gated.astype(BF16)]
    broadcast_in_dim x0 -> x1, local copies, waits for them, and re-layouts: none -> 1.33 us  [shards(): gains = jnp.broadcast_to(skip_gain[:, None], (channels, 128))]
where the time goes in v1:
time: 82.2 us; the launch traced here: 82 us
  Pallas kernels  78.4 us (95%)
  local copies, waits for them, and re-layouts  3.59 us (4%)
    pallas_call x1, Pallas kernels, shards(): pl.pallas_call(functools.partial(kernel, devices, chunk, fused), out_shap...  78.4 us
    unnamed x1, local copies, waits for them, and re-layouts  2.26 us

profile of v1, /device:TPU:1, one launch (start us, length us, event | category | flops | bytes accessed | tf_op | source)
XLA Modules:
  0.0 82.0 jit_solution(673496733437413450)
XLA Ops:
  0.0 1.3 %broadcast_in_dim.2.refs_10_ = f32[32,128]{1,0:T(8,128)} broadcast(f32[32]{0:T(128)} %param.14), dimensions={0} | broadcast | bytes 16512 | tf_op jit(solution)/shard_map/broadcast_in_dim | solution.py:299
  1.3 78.4 %shard_map.109 = bf16[32,16384]{1,0:T(8,128)(2,1)} custom-call(bf16[2,512,512]{2,1,0:T(8,128)(2,1)} %constant.14.clone.refs_0_, bf16[2,512,512]{2,1,0:T(8,128)(2,1)} %constant.15.clone.refs_1_, bf16[2,512,512]{2,1,0:T(8,128)(2,1)} %constant.16.clone.refs_2_, bf16[2,512,512]{2,1,0:T(8,128)(2,1)} %constant.17.clone.refs_3_, ...), custom_call_target="tpu_custom_call" | custom-call | tf_op jit(solution)/shard_map/pallas_call | solution.py:308
  79.7 2.3 %copy.13 = bf16[32,16384]{1,0:T(8,128)(2,1)} copy(bf16[32,16384]{1,0:T(8,128)(2,1)} %shard_map.109) | data formatting | bytes 2097152
